TPU v7x, 256 devices: a whole 4x4x8 slice. The times are simulated.
256 devices in a mesh: section: 4 (over y), row: 16 (over z, core), col: 4 (over x).
Axes of the slice: x: 4, y: 4, z: 8, core: 2. Of those that a mesh axis runs over, the one named last changes fastest.
Arguments:
- inputs: bfloat16 [1024, 12288], P('section', ('col', 'row')), may hold values from -6 to 6
- out_grad: bfloat16 [1024, 12288], P('section', ('col', 'row')), may hold values from -1.5 to 1.5
- w_up: bfloat16 [12288, 24576], P('col', ('section', 'row')), may hold values from -0.0546875 to 0.0546875
- w_down: bfloat16 [12288, 24576], P('col', ('section', 'row')), may hold values from -0.0546875 to 0.0546875
Outputs:
- input_grad: float32 [1024, 12288], P('section', ('col', 'row'))
- w_up_grad: bfloat16 [12288, 24576], P('col', ('section', 'row'))
- w_down_grad: bfloat16 [12288, 24576], P('col', ('section', 'row'))
All inputs are finite; a program needn't handle non-finite values.
Results may differ from a plain program's by a relative error of at most 0.02.
Values may be sent and summed in bfloat16 or wider, within the bound.
A program may use at most 192 MiB of HBM per device.

v0:
```python
import jax
import jax.numpy as jnp
from jax import lax
from jax.sharding import PartitionSpec as P

coeff = 0.7978845608028654


def gelu_pair(pre, back):
    inner = coeff * (pre + 0.044715 * pre * pre * pre)
    tanh_val = jnp.tanh(inner)
    act = 0.5 * pre * (1.0 + tanh_val)
    slope = 0.5 * (1.0 + tanh_val) + 0.5 * pre * (1.0 - tanh_val * tanh_val) * coeff * (
        1.0 + 3.0 * 0.044715 * pre * pre
    )
    return (act.astype(jnp.bfloat16), (back * slope).astype(jnp.bfloat16))


def token_sum(left, right):
    return lax.dot_general(
        left, right, (((0,), (0,)), ((), ())), preferred_element_type=jnp.float32
    )


def on_device(inputs, out_grad, w_up, w_down):
    x_wide, dy_wide = (
        lax.all_gather(inputs, "row", axis=1, tiled=True),
        lax.all_gather(out_grad, "row", axis=1, tiled=True),
    )
    x_all, dy_all = (
        lax.all_gather(x_wide, "section", axis=0, tiled=True),
        lax.all_gather(dy_wide, "section", axis=0, tiled=True),
    )
    pre_part = jnp.dot(x_all, w_up, preferred_element_type=jnp.float32)
    back_part = jnp.dot(dy_all, w_down, preferred_element_type=jnp.float32)
    pre, back = (
        lax.psum_scatter(
            pre_part.astype(jnp.bfloat16), "col", scatter_dimension=0, tiled=True
        ).astype(jnp.float32),
        lax.psum_scatter(
            back_part.astype(jnp.bfloat16), "col", scatter_dimension=0, tiled=True
        ).astype(jnp.float32),
    )
    act, grad_pre = gelu_pair(pre, back)
    act_all, grad_all = (
        lax.all_gather(act, "col", axis=0, tiled=True),
        lax.all_gather(grad_pre, "col", axis=0, tiled=True),
    )
    w_down_grad = token_sum(dy_all, act_all).astype(jnp.bfloat16)
    w_up_grad = token_sum(x_all, grad_all).astype(jnp.bfloat16)
    own_rows = inputs.shape[0]
    piece_width = inputs.shape[1]
    n_rows = lax.axis_size("row")
    blocks = lax.axis_size(("section", "row")) * own_rows // own_rows
    targets = jnp.arange(blocks, dtype=jnp.int32)

    def one_target(target):
        rows = lax.dynamic_slice_in_dim(grad_all, target // n_rows * own_rows, own_rows, 0)
        cols = lax.dynamic_slice_in_dim(w_up, target % n_rows * piece_width, piece_width, 0)
        return lax.dot_general(
            rows, cols, (((1,), (1,)), ((), ())), preferred_element_type=jnp.float32
        )

    input_grad = lax.psum_scatter(
        jax.vmap(one_target)(targets).reshape(
            lax.axis_size(("section", "row")) * own_rows, piece_width
        ),
        ("section", "row"),
        scatter_dimension=0,
        tiled=True,
    )
    return (input_grad, w_up_grad, w_down_grad)


def solution(mesh):
    return jax.shard_map(
        on_device,
        mesh=mesh,
        in_specs=(
            P("section", ("col", "row")),
            P("section", ("col", "row")),
            P("col", ("section", "row")),
            P("col", ("section", "row")),
        ),
        out_specs=(
            P("section", ("col", "row")),
            P("col", ("section", "row")),
            P("col", ("section", "row")),
        ),
        check_vma=False,
    )
```

profile of v0, /device:TPU:2, one launch (start us, length us, event | category | flops | bytes accessed | tf_op | source)
XLA Modules:
  0.0 753.1 jit_solution(985175644298660991)
XLA Ops:
  8.7 43.2 %all-gather.5.cloned.1.call-done = bf16[256,3072]{0,1:T(8,128)(2,1)} async-done(((bf16[256,192]{0,1:T(8,128)(2,1)}), bf16[256,3072]{0,1:T(8,128)(2,1)}) %all-gather.5.cloned.1.call-update) | async-done | bytes 1572880 | tf_op jit(solution)/shard_map/all_gather | solution.py:28
  52.0 39.6 %all-gather.9.cloned.1.call-done = bf16[256,3072]{0,1:T(8,128)(2,1)} async-done(((bf16[256,192]{0,1:T(8,128)(2,1)}), bf16[256,3072]{0,1:T(8,128)(2,1)}) %all-gather.9.cloned.1.call-update) | async-done | bytes 1572880 | tf_op jit(solution)/shard_map/all_gather | solution.py:27
  91.7 72.8 %all-gather.7.cloned.1.call-done = bf16[1024,3072]{0,1:T(8,128)(2,1)} async-done(((bf16[256,3072]{0,1:T(8,128)(2,1)}), bf16[1024,3072]{0,1:T(8,128)(2,1)}) %all-gather.7.cloned.1.call-update) | async-done | bytes 6291472 | tf_op jit(solution)/shard_map/all_gather | solution.py:32
  164.4 6.5 convolution_convert_fusion.3
  171.0 68.0 %all-gather.11.cloned.1.call-done = bf16[1024,3072]{0,1:T(8,128)(2,1)} async-done(((bf16[256,3072]{0,1:T(8,128)(2,1)}), bf16[1024,3072]{0,1:T(8,128)(2,1)}) %all-gather.11.cloned.1.call-update) | async-done | bytes 6291472 | tf_op jit(solution)/shard_map/all_gather | solution.py:31
  239.0 7.8 %convolution_convert_fusion.2 = bf16[1024,384]{1,0:T(8,128)(2,1)} fusion(bf16[1024,3072]{0,1:T(8,128)(2,1)} %all-gather.11.cloned.1.call-done, bf16[3072,384]{1,0:T(8,128)(2,1)} %param.6), kind=kOutput, calls=%fused_computation.9 | convolution fusion | flops 2416312320 | bytes 9437184 | tf_op jit(solution)/shard_map/dot_general | solution.py:34
  246.9 173.9 %while.3 = (s32[]{:T(128)}, bf16[3072,384]{1,0:T(8,128)(2,1)}, s32[64,2]{0,1:T(2,128)S(1)}, bf16[64,192,384]{2,1,0:T(8,128)(2,1)}, s32[]{:T(128)}) while((s32[]{:T(128)}, bf16[3072,384]{1,0:T(8,128)(2,1)}, s32[64,2]{0,1:T(2,128)S(1)}, bf16[64,192,384]{2,1,0:T(8,128)(2,1)}, s32[]{:T(128)}) %tuple.37), condition=%wide.while_cond.1, body=%wide.while_body.1.sunk | while | flops 2 | bytes 295525 | solution.py:59
  252.9 2.2 bitcast_dynamic-update-slice_fusion.5
  258.4 2.2 bitcast_dynamic-update-slice_fusion.5
  280.1 2.2 bitcast_dynamic-update-slice_fusion.5
  291.0 2.2 bitcast_dynamic-update-slice_fusion.5
  358.9 2.2 bitcast_dynamic-update-slice_fusion.5
  405.1 2.2 bitcast_dynamic-update-slice_fusion.5
  410.5 2.2 bitcast_dynamic-update-slice_fusion.5
  422.2 14.1 %all_gather.22 = bf16[1024,384]{1,0:T(8,128)(2,1)S(1)} all-gather(bf16[256,384]{1,0:T(8,128)(2,1)S(1)} %get-tuple-element.42), channel_id=1, replica_groups=mesh['section'=4,'row'=16,'col'=4] {'col'}, dimensions={0}, use_global_device_ids=true | all-gather | bytes 983040 | tf_op jit(solution)/shard_map/all_gather | solution.py:47
  436.4 125.7 %while.2 = (s32[]{:T(128)}, bf16[1024,384]{1,0:T(8,128)(2,1)S(1)}, s32[64,2]{0,1:T(2,128)S(1)}, bf16[64,256,384]{2,1,0:T(8,128)(2,1)}, s32[]{:T(128)}) while((s32[]{:T(128)}, bf16[1024,384]{1,0:T(8,128)(2,1)S(1)}, s32[64,2]{0,1:T(2,128)S(1)}, bf16[64,256,384]{2,1,0:T(8,128)(2,1)}, s32[]{:T(128)}) %tuple.34), condition=%wide.while_cond, body=%wide.while_body.sunk | while | flops 2 | bytes 393829 | solution.py:58
  562.1 12.2 %convolution_bitcast_fusion = f32[64,24,8,256]{3,2,1,0:T(8,128)} fusion(bf16[64,256,384]{2,1,0:T(8,128)(2,1)} %get-tuple-element.10, bf16[64,192,384]{2,1,0:T(8,128)(2,1)} %get-tuple-element.18), kind=kOutput, calls=%fused_computation.4 | convolution fusion | flops 2415919104 | bytes 34603008 | tf_op jit(solution)/shard_map/vmap()/dot_general | solution.py:60
  574.3 10.7 %copy.12 = f32[64,24,8,256]{3,2,0,1:T(8,128)} copy(f32[64,24,8,256]{3,2,1,0:T(8,128)} %convolution_bitcast_fusion) | data formatting | bytes 25165824 | tf_op jit(solution)/shard_map/reshape | solution.py:65
  585.0 14.5 %all_gather.23 = bf16[1024,384]{1,0:T(8,128)(2,1)S(1)} all-gather(bf16[256,384]{1,0:T(8,128)(2,1)S(1)} %get-tuple-element.41), channel_id=1, replica_groups=mesh['section'=4,'row'=16,'col'=4] {'col'}, dimensions={0}, use_global_device_ids=true | all-gather | bytes 983040 | tf_op jit(solution)/shard_map/all_gather | solution.py:46
  599.5 7.1 fusion.1
  606.7 4.5 copy.11
  611.2 7.1 fusion
  618.2 4.3 copy.10
  622.6 123.6 %reduce-scatter.8.cloned.1.call-done = f32[256,192]{0,1:T(8,128)} async-done(((f32[16384,192]{0,1:T(8,128)}), f32[256,192]{0,1:T(8,128)}) %reduce-scatter.8.cloned.1.call-update) | async-done | bytes 196624 | tf_op jit(solution)/shard_map/reduce_scatter | solution.py:64
  (404 shorter events, 287.4 us)
Async XLA Ops:
  7.2 157.3 %copy-start = (bf16[3072,384]{1,0:T(8,128)(2,1)S(1)}, bf16[3072,384]{1,0:T(8,128)(2,1)}, u32[]{:S(2)}) copy-start(bf16[3072,384]{1,0:T(8,128)(2,1)} %param.7) | copy-start | bytes 7077892
  7.2 44.8 %all-gather.5.cloned.1.call-start = ((), (), s32[]{:S(2)}) async-start(), calls=%async_computation.3 | async-start | bytes 1671168 | tf_op jit(solution)/shard_map/all_gather | solution.py:28
  7.9 83.7 %all-gather.9.cloned.1.call-start = ((), (), s32[]{:S(2)}) async-start(), calls=%async_computation.6 | async-start | bytes 1671168 | tf_op jit(solution)/shard_map/all_gather | solution.py:27
  8.7 155.8 %all-gather.7.cloned.1.call-start = ((), (), s32[]{:S(2)}) async-start(), calls=%async_computation.4 | async-start | bytes 7864320 | tf_op jit(solution)/shard_map/all_gather | solution.py:32
  52.0 187.1 %all-gather.11.cloned.1.call-start = ((), (), s32[]{:S(2)}) async-start(), calls=%async_computation.7 | async-start | bytes 7864320 | tf_op jit(solution)/shard_map/all_gather | solution.py:31
  91.6 329.2 %reduce-scatter.4.cloned.1.call-start = ((), (), s32[]{:S(2)}) async-start(), calls=%async_computation.5 | async-start | bytes 983040 | tf_op jit(solution)/shard_map/reduce_scatter | solution.py:40
  171.0 249.9 %reduce-scatter.6.cloned.1.call-start = ((), (), s32[]{:S(2)}) async-start(), calls=%async_computation.8 | async-start | bytes 983040 | tf_op jit(solution)/shard_map/reduce_scatter | solution.py:37
  246.9 499.3 %reduce-scatter.8.cloned.1.call-start = ((), (), s32[]{:S(2)}) async-start(), calls=%async_computation.9 | async-start | bytes 12779520 | tf_op jit(solution)/shard_map/reduce_scatter | solution.py:64
  606.7 139.6 %copy-start.1 = (bf16[3072,384]{1,0:T(8,128)(2,1)S(1)}, bf16[3072,384]{1,0:T(8,128)(2,1)}, u32[]{:S(2)}) copy-start(bf16[3072,384]{1,0:T(8,128)(2,1)} %param.7) | copy-start | bytes 7077892
Sparse Core Ops, SparseCore 0:
  9.8 42.0 all-gather.4
  53.8 37.7 all-gather.8
  93.4 70.9 all-gather.6
  166.1 72.9 all-gather.10
  242.0 23.3 reduce-scatter.3
  268.4 24.6 reduce-scatter.5
  585.1 161.0 reduce-scatter.7
where the time goes:
time: 756 us; the launch traced here: 753 us
  waiting for transfers between devices  349 us (46%)
  local copies, waits for them, and re-layouts  319 us (42%)
  matrix products  40.7 us (5%)
  blocking collectives  28.7 us (4%)
  between operations  14.2 us (2%)
    gather x384, local copies, waits for them, and re-layouts  299 us
    reduce_scatter x1, waiting for transfers between devices, on_device(): lax.psum_scatter(jax.vmap(one_target)(targets).reshape(lax.axis_size(('se...  124 us
    all_gather x1, waiting for transfers between devices, on_device(): lax.all_gather(dy_wide, 'section', axis=0, tiled=True)  72.8 us
    all_gather x1, waiting for transfers between devices, on_device(): lax.all_gather(x_wide, 'section', axis=0, tiled=True)  68 us
    all_gather x1, waiting for transfers between devices, on_device(): lax.all_gather(out_grad, 'row', axis=1, tiled=True)  43.2 us
    all_gather x1, waiting for transfers between devices, on_device(): lax.all_gather(inputs, 'row', axis=1, tiled=True)  39.6 us
  transfers between devices with their start and end apart: 7, of which 5 were waited for; matrix products, arithmetic and copies ran while one was open for 28% of the time, Pallas kernels for 0%

commit v1 on v0

v1 whole, which is shorter than its diff:
```python
import functools

import jax
import jax.numpy as jnp
from jax import lax
from jax.experimental import pallas as pl
from jax.experimental.pallas import tpu as pltpu
from jax.sharding import PartitionSpec as P

coeff = 0.7978845608028654
f32 = jnp.float32
bf16 = jnp.bfloat16
R, L = 0, 1
N_SEMS = 224

Z_REL = (0, 1, -1, 2, -2, 3, -3, 4)
GATHER_SRC = {R: (0, 2, 4, 6), L: (0, 1, 3, 5)}
GATHER_DST = {R: (2, 4, 6, 7), L: (1, 3, 5, 7)}
GROUPS = {1: (0, 3), 2: (3, 5), 3: (5, 7), 4: (7, 8)}
SUM_SRC = {R: (7, 5, 3, 1), L: (7, 6, 4, 2)}
SUM_DST = {R: (5, 3, 1, 0), L: (6, 4, 2, 0)}


def gelu_pair(pre, back):
    inner = coeff * (pre + 0.044715 * pre * pre * pre)
    tanh_val = jnp.tanh(inner)
    act = 0.5 * pre * (1.0 + tanh_val)
    slope = 0.5 * (1.0 + tanh_val) + 0.5 * pre * (1.0 - tanh_val * tanh_val) * coeff * (
        1.0 + 3.0 * 0.044715 * pre * pre
    )
    return act, back * slope


def kernel(
    x_in, d_in, wu_in, wd_in,
    ig_out, gu_out, gd_out,
    X, D, WU, UT, DT, WG, PB, RL, FN, AGB, AT, IGP, CR, ZR, YR, YF,
    send_sems, recv_sems, local_sems,
):
    n_sec, n_row, n_col = (lax.axis_size(a) for a in ("section", "row", "col"))
    n_z = n_row // 2
    s, r, c = (lax.axis_index(a) for a in ("section", "row", "col"))
    z, core = r // 2, r % 2

    def turn(i, by, n):
        return lax.rem(i + (by + n), n)

    zdev = {d: {"row": turn(z, by, n_z) * 2 + core} for d, by in ((R, 1), (L, -1))}
    ydev = {d: {"section": turn(s, by, n_sec)} for d, by in ((R, 1), (L, -1))}
    xdev = {d: {"col": turn(c, by, n_col)} for d, by in ((R, 1), (L, -1))}
    partner = {"row": z * 2 + (1 - core)}

    barrier = pltpu.get_barrier_semaphore()
    for dev in (*zdev.values(), *ydev.values(), *xdev.values(), partner):
        pl.semaphore_signal(
            barrier, inc=1, device_id=dev, device_id_type=pl.DeviceIdType.MESH
        )

    own_x = pltpu.make_async_copy(x_in, X.at[0, 0, 0], local_sems.at[0])
    own_d = pltpu.make_async_copy(d_in, D.at[0, 0, 0], local_sems.at[1])
    own_x.start()
    own_d.start()
    WD = WG.at[1]

    def block_rows(slot, other):
        row = turn(z, Z_REL[slot], n_z) * 2 + (1 - core if other else core)
        return pl.ds(pl.multiple_of(row * 192, 192), 192)

    for src, dst, sem in ((wu_in, WU, 2), (wd_in, WD, 3)):
        for slot in range(8):
            for other in range(2):
                pltpu.make_async_copy(
                    src.at[block_rows(slot, other)], dst.at[slot, other], local_sems.at[sem]
                ).start()

    pl.semaphore_wait(barrier, 7)

    started = {}
    arrived = set()

    def start(name, src, dst, dev):
        i = len(started)
        assert i < N_SEMS and name not in started
        started[name] = pltpu.make_async_remote_copy(
            src_ref=src,
            dst_ref=dst,
            send_sem=send_sems.at[i],
            recv_sem=recv_sems.at[i],
            device_id=dev,
            device_id_type=pl.DeviceIdType.MESH,
        )
        started[name].start()

    def need(*names):
        for name in names:
            if name not in arrived:
                arrived.add(name)
                started[name].wait_recv()

    bufs = {"X": X, "D": D}
    far_dir = {("X", 0): R, ("D", 0): L, ("D", 1): R, ("D", 2): L, ("D", 3): R}

    def zsend(nm, k, h, src=None):
        for d in (R, L):
            if h < 4 or far_dir[nm, k] == d:
                b = bufs[nm]
                a = b.at[k, GATHER_SRC[d][h - 1], 0] if src is None else src
                start(f"{nm}{k}z{h}{d}", a, b.at[k, GATHER_DST[d][h - 1], 0], zdev[d])

    def zgot(nm, k, h):
        for d in (R, L):
            if h < 4 or far_dir[nm, k] == d:
                need(f"{nm}{k}z{h}{d}")
        if h < 4:
            zsend(nm, k, h + 1)
        lo, hi = GROUPS[h]
        b = bufs[nm]
        if nm == "X":
            start(f"Xy{h}{R}", X.at[0, lo:hi, 0], X.at[2, lo:hi, 0], ydev[R])
            start(f"Xy{h}{L}", X.at[0, lo:hi, 0], X.at[1, lo:hi, 0], ydev[L])
        start(f"{nm}{k}c{h}", b.at[k, lo:hi, 0], b.at[k, lo:hi, 1], partner)

    def ygot(h):
        need(f"Xy{h}{R}", f"Xy{h}{L}")
        lo, hi = GROUPS[h]
        if h == 1:
            start("Xf0", X.at[2, 0:3, 0], X.at[3, 0:3, 0], ydev[R])
        if h == 3:
            start("Xf1", X.at[1, 3:7, 0], X.at[3, 3:7, 0], ydev[L])
        if h == 4:
            start("Xf2", X.at[2, 7:8, 0], X.at[3, 7:8, 0], ydev[R])
        start(f"Xyc{h}", X.at[1:3, lo:hi, 0], X.at[1:3, lo:hi, 1], partner)

    def fgot(i):
        need(f"Xf{i}")
        lo, hi = ((0, 3), (3, 7), (7, 8))[i]
        start(f"Xfc{i}", X.at[3, lo:hi, 0], X.at[3, lo:hi, 1], partner)

    def transpose(src, dst):
        @pl.loop(0, 4)
        def _(p):
            dst[p] = src[pl.ds(p * 2, 2)].reshape(768, 384).T

    def hidden(owner):
        return pl.ds(pl.multiple_of(owner * 96, 96), 96)

    c_next, c_prev, c_far = turn(c, 1, n_col), turn(c, -1, n_col), turn(c, 2, n_col)

    def partial(k):
        if k == 0:
            need(*(f"{nm}0c{h}" for nm in "XD" for h in (1, 2, 3, 4)))
        elif k < 3:
            need(*(f"Xyc{h}" for h in (1, 2, 3, 4)))
            need(*(f"D{k}c{h}" for h in (1, 2, 3, 4)))
        else:
            need(*(f"Xfc{i}" for i in range(3)))
            need(*(f"D{k}c{h}" for h in (1, 2, 3, 4)))
        for j, (b, w) in enumerate(((X, UT), (D, DT))):
            acc = jnp.zeros((384, 256), f32)
            for p in range(4):
                acc += jnp.dot(
                    w[p], b[k, 2 * p : 2 * p + 2].reshape(768, 256), preferred_element_type=f32
                )
            PB[k, j] = acc.astype(bf16)
        start(f"r{k}{R}", PB.at[k, 0, hidden(c_far)], RL.at[k, 0], xdev[R])
        start(f"r{k}{L}", PB.at[k, 1, hidden(c_far)], RL.at[k, 1], xdev[L])
        start(f"f{k}b{R}", PB.at[k, 1, hidden(c_next)], FN.at[k, 0, 1], xdev[R])
        start(f"f{k}p{L}", PB.at[k, 0, hidden(c_prev)], FN.at[k, 1, 0], xdev[L])

    def relay(k):
        for j, d, rows, tag in ((0, R, hidden(c_next), "p"), (1, L, hidden(c_prev), "b")):
            need(f"r{k}{d}")
            PB[k, j, rows] = (PB[k, j, rows].astype(f32) + RL[k, j].astype(f32)).astype(bf16)
            start(f"f{k}{tag}{d}", PB.at[k, j, rows], FN.at[k, d, j], xdev[d])

    def gelu(k):
        need(*(f"f{k}{tag}{d}" for tag in "pb" for d in (R, L)))
        rows = hidden(c)
        pre, back = (
            PB[k, j, rows].astype(f32) + FN[k, 0, j].astype(f32) + FN[k, 1, j].astype(f32)
            for j in range(2)
        )
        act, grad = gelu_pair(pre, back)
        AGB[k, 0, rows] = act.astype(bf16)
        AGB[k, 1, rows] = grad.astype(bf16)
        for d in (R, L):
            start(f"a{k}{d}", AGB.at[k, :, rows], AGB.at[k, :, rows], xdev[d])

    def spread(k):
        need(f"a{k}{R}")
        rows = hidden(c_prev)
        start(f"h{k}{R}", AGB.at[k, 0, rows], AGB.at[k, 0, rows], xdev[R])
        need(f"a{k}{L}")
        rows = hidden(c_next)
        start(f"h{k}{L}", AGB.at[k, 1, rows], AGB.at[k, 1, rows], xdev[L])

    def ig_part(k):
        need(f"h{k}{R}", f"h{k}{L}")

        @pl.loop(0, 4)
        def _(p):
            w = WU[pl.ds(p * 2, 2)].reshape(768, 384)
            g = jnp.dot(w, AGB[k, 1], preferred_element_type=f32)
            IGP[k, pl.ds(p * 2, 2)] = g.astype(bf16).reshape(2, 2, 192, 256)

        start(f"C{k}", IGP.at[k, :, 1], CR.at[k], partner)

    def sum_hops(k, d):
        return (0, 1, 2, 3) if (k % 2 == 0) == (d == R) else (1, 2, 3)

    def zsum_send(k, d, j):
        start(f"S{k}{d}{j}", IGP.at[k, SUM_SRC[d][j], 0], ZR.at[k, d, j], zdev[d])

    def core_sum(k):
        need(f"C{k}")
        for slot in (7, 6, 5, 4, 3, 2, 1, 0):
            IGP[k, slot, 0] = (IGP[k, slot, 0].astype(f32) + CR[k, slot].astype(f32)).astype(bf16)
            for d in (R, L):
                j = sum_hops(k, d)[0]
                if SUM_SRC[d][j] == slot:
                    zsum_send(k, d, j)

    def zsum(k, j):
        for d in (R, L):
            if j in sum_hops(k, d):
                need(f"S{k}{d}{j}")
                slot = SUM_DST[d][j]
                if j < 3:
                    IGP[k, slot, 0] = (
                        IGP[k, slot, 0].astype(f32) + ZR[k, d, j].astype(f32)
                    ).astype(bf16)
                    zsum_send(k, d, j + 1)

    lower, upper = slice(0, 96), slice(96, 192)

    def zsum_end(k):
        zsum(k, 3)
        total = IGP[k, 0, 0].astype(f32) + ZR[k, 0, 3].astype(f32) + ZR[k, 1, 3].astype(f32)
        if k == 0:
            ig_out[...] = total
            return
        IGP[k, 0, 0] = total.astype(bf16)
        if k == 1:
            start("yfb", IGP.at[1, 0, 0, upper], YF.at[0, upper], ydev[R])
        elif k == 2:
            start("yfc", IGP.at[2, 0, 0, lower], YF.at[1, lower], ydev[L])
        else:
            start("yr0", IGP.at[3, 0, 0, lower], YR.at[0], ydev[R])
            start("yr1", IGP.at[3, 0, 0, upper], YR.at[1], ydev[L])

    def ysum():
        for d, k, part in ((R, 1, lower), (L, 2, upper)):
            need(f"yr{d}")
            IGP[k, 0, 0, part] = (
                IGP[k, 0, 0, part].astype(f32) + YR[d].astype(f32)
            ).astype(bf16)
            start(f"yf{d}", IGP.at[k, 0, 0, part], YF.at[d, part], ydev[d])

    def ysum_end():
        need("yfb", "yfc", "yf0", "yf1")
        ig_out[...] = ig_out[...] + YF[0].astype(f32) + YF[1].astype(f32)

    def turn_acts():
        for k in range(4):
            for j in range(2):
                AT[j, k] = AGB[k, j].T

    def weight_grad(which, slots):
        b, j, out = ((X, 1, gu_out), (D, 0, gd_out))[which]
        for slot in slots:
            acc = jnp.zeros((384, 384), f32)
            for k in range(4):
                acc += jnp.dot(
                    b[k, slot].reshape(384, 256), AT[j, k], preferred_element_type=f32
                )
            WG[which, slot] = acc.astype(bf16).reshape(2, 192, 384)
            for other in range(2):
                pltpu.make_async_copy(
                    WG.at[which, slot, other],
                    out.at[block_rows(slot, other)],
                    local_sems.at[4 + which],
                ).start()

    zsend("X", 0, 1, x_in)
    zsend("D", 0, 1, d_in)
    start("Dy0", d_in, D.at[2, 0, 0], ydev[R])
    start("Dy1", d_in, D.at[1, 0, 0], ydev[L])
    own_x.wait()
    own_d.wait()
    pltpu.make_async_copy(WU, WU, local_sems.at[2]).wait()
    transpose(WU, UT)
    zgot("X", 0, 1)
    zgot("D", 0, 1)
    need("Dy0", "Dy1")
    start("Dy2", D.at[2, 0, 0], D.at[3, 0, 0], ydev[R])
    pltpu.make_async_copy(WD, WD, local_sems.at[3]).wait()
    transpose(WD, DT)
    zgot("X", 0, 2)
    zgot("D", 0, 2)
    zsend("D", 1, 1)
    ygot(1)
    need("Dy2")
    zgot("X", 0, 3)
    zgot("D", 0, 3)
    zgot("D", 1, 1)
    zsend("D", 2, 1)
    ygot(2)
    zgot("X", 0, 4)
    zgot("D", 0, 4)
    zgot("D", 1, 2)
    zgot("D", 2, 1)
    ygot(3)
    fgot(0)
    partial(0)
    zgot("D", 1, 3)
    zgot("D", 2, 2)
    zsend("D", 3, 1)
    ygot(4)
    relay(0)
    zgot("D", 1, 4)
    zgot("D", 2, 3)
    zgot("D", 3, 1)
    gelu(0)
    fgot(1)
    partial(1)
    zgot("D", 2, 4)
    zgot("D", 3, 2)
    spread(0)
    relay(1)
    partial(2)
    fgot(2)
    zgot("D", 3, 3)
    ig_part(0)
    gelu(1)
    relay(2)
    zgot("D", 3, 4)
    core_sum(0)
    spread(1)
    partial(3)
    gelu(2)
    zsum(0, 0)
    ig_part(1)
    relay(3)
    zsum(0, 1)
    core_sum(1)
    spread(2)
    zsum(0, 2)
    gelu(3)
    ig_part(2)
    zsum(1, 0)
    zsum_end(0)
    core_sum(2)
    spread(3)
    zsum(1, 1)
    zsum(2, 0)
    ig_part(3)
    zsum(1, 2)
    zsum(2, 1)
    core_sum(3)
    turn_acts()
    zsum_end(1)
    zsum(2, 2)
    weight_grad(0, (0, 1))
    zsum(3, 0)
    zsum_end(2)
    weight_grad(0, (2, 3, 4))
    zsum(3, 1)
    weight_grad(0, (5, 6, 7))
    zsum(3, 2)
    weight_grad(1, (0, 1, 2))
    zsum_end(3)
    weight_grad(1, (3, 4, 5))
    ysum()
    weight_grad(1, (6, 7))
    ysum_end()
    assert arrived == set(started)
    for copy in started.values():
        copy.wait_send()
    for which in range(2):
        pltpu.make_async_copy(WG.at[which], WG.at[which], local_sems.at[4 + which]).wait()


def on_device(inputs, out_grad, w_up, w_down):
    any_spec = pl.BlockSpec(memory_space=pl.ANY)
    ig_t, gu, gd = pl.pallas_call(
        kernel,
        out_shape=(
            jax.ShapeDtypeStruct((192, 256), f32),
            jax.ShapeDtypeStruct((3072, 384), bf16),
            jax.ShapeDtypeStruct((3072, 384), bf16),
        ),
        in_specs=[any_spec] * 4,
        out_specs=(pl.BlockSpec(memory_space=pltpu.VMEM), any_spec, any_spec),
        scratch_shapes=[
            pltpu.VMEM((4, 8, 2, 192, 256), bf16),
            pltpu.VMEM((4, 8, 2, 192, 256), bf16),
            pltpu.VMEM((8, 2, 192, 384), bf16),
            pltpu.VMEM((4, 384, 768), bf16),
            pltpu.VMEM((4, 384, 768), bf16),
            pltpu.VMEM((2, 8, 2, 192, 384), bf16),
            pltpu.VMEM((4, 2, 384, 256), bf16),
            pltpu.VMEM((4, 2, 96, 256), bf16),
            pltpu.VMEM((4, 2, 2, 96, 256), bf16),
            pltpu.VMEM((4, 2, 384, 256), bf16),
            pltpu.VMEM((2, 4, 256, 384), bf16),
            pltpu.VMEM((4, 8, 2, 192, 256), bf16),
            pltpu.VMEM((4, 8, 192, 256), bf16),
            pltpu.VMEM((4, 2, 4, 192, 256), bf16),
            pltpu.VMEM((2, 96, 256), bf16),
            pltpu.VMEM((2, 192, 256), bf16),
            pltpu.SemaphoreType.DMA((N_SEMS,)),
            pltpu.SemaphoreType.DMA((N_SEMS,)),
            pltpu.SemaphoreType.DMA((6,)),
        ],
        compiler_params=pltpu.CompilerParams(
            collective_id=0, has_side_effects=True, vmem_limit_bytes=58 * 2**20
        ),
        cost_estimate=pl.CostEstimate(
            flops=5 * 2 * 1024 * 3072 * 384, bytes_accessed=10_000_000, transcendentals=98304
        ),
        name="ffn_backward",
    )(inputs.T, out_grad.T, w_up, w_down)
    return ig_t.T, gu, gd


def solution(mesh):
    return jax.shard_map(
        on_device,
        mesh=mesh,
        in_specs=(
            P("section", ("col", "row")),
            P("section", ("col", "row")),
            P("col", ("section", "row")),
            P("col", ("section", "row")),
        ),
        out_specs=(
            P("section", ("col", "row")),
            P("col", ("section", "row")),
            P("col", ("section", "row")),
        ),
        check_vma=False,
    )
```

time: 756 us -> 124 us (0.16)
  waiting for transfers between devices: 349 us -> 0 us
  local copies, waits for them, and re-layouts: 319 us -> 6.48 us
  Pallas kernels: 0 us -> 117 us
  matrix products: 40.7 us -> 0 us
  blocking collectives: 28.7 us -> 0 us
  between operations: 14.2 us -> 0.64 us
    gather x384 -> x0, local copies, waits for them, and re-layouts: 299 us -> none
    all_gather x4 -> x0, waiting for transfers between devices: 224 us -> none  [the longest x1 72.8 us: on_device(): lax.all_gather(dy_wide, 'section', axis=0, tiled=True)]
    reduce_scatter x3 -> x0, waiting for transfers between devices: 124 us -> none  [the longest x1 124 us: on_device(): lax.psum_scatter(jax.vmap(one_target)(targets).reshape(lax.axis_size(('se...]
    pallas_call x0 -> x1, Pallas kernels: none -> 117 us  [on_device(): pl.pallas_call(kernel, out_shape=(jax.ShapeDtypeStruct((192, 256), f32),...]
    dot_general x5 -> x0, matrix products: 40.7 us -> none  [the longest x2 14.2 us: token_sum(): lax.dot_general(left, right, (((0,), (0,)), ((), ())), preferred_element_...]
    all_gather x2 -> x0, blocking collectives: 28.7 us -> none  [the longest x1 14.5 us: on_device(): lax.all_gather(act, 'col', axis=0, tiled=True)]
    reshape x1 -> x0, local copies, waits for them, and re-layouts: 10.7 us -> none  [on_device(): jax.vmap(one_target)(targets)]
  transfers between devices with their start and end apart: 7 -> 0, of which waited for: 5 -> 0; matrix products, arithmetic and copies ran while one was open for 28% -> 0% of each run, Pallas kernels for 0% -> 0%
where the time goes in v1:
time: 124 us
  Pallas kernels  117 us (94%)
  local copies, waits for them, and re-layouts  6.48 us (5%)
    pallas_call x1, Pallas kernels, on_device(): pl.pallas_call(kernel, out_shape=(jax.ShapeDtypeStruct((192, 256), f32),...  117 us
    unnamed x5, local copies, waits for them, and re-layouts  6.48 us

profile of v1, /device:TPU:2, one launch (start us, length us, event | category | flops | bytes accessed | tf_op | source)
XLA Modules:
  0.0 124.0 jit_solution(18373391436791908799)
XLA Ops:
  0.6 116.9 %ffn_backward.1 = (f32[192,256]{1,0:T(8,128)}, bf16[3072,384]{1,0:T(8,128)(2,1)}, bf16[3072,384]{1,0:T(8,128)(2,1)}) custom-call(bf16[192,256]{1,0:T(8,128)(2,1)} %bitcast.4, bf16[192,256]{1,0:T(8,128)(2,1)} %bitcast.5, bf16[3072,384]{1,0:T(8,128)(2,1)} %wu_in.1, bf16[3072,384]{1,0:T(8,128)(2,1)} %wd_in.1), custom_call_target="tpu_custom_call" | custom-call | flops 12079595520 | bytes 10000000 | tf_op jit(solution)/shard_map/ffn_backward/pallas_call | solution.py:385
  117.5 1.6 %copy.10 = f32[256,192]{0,1:T(8,128)} copy(f32[256,192]{0,1:T(8,128)} %bitcast.3) | data formatting | bytes 393216
  119.1 0.0 copy-start
  119.1 3.5 %copy.11 = bf16[3072,384]{1,0:T(8,128)(2,1)} copy(bf16[3072,384]{1,0:T(8,128)(2,1)} %get-tuple-element.13) | data formatting | bytes 4718592
  122.6 0.0 copy-done
  122.6 1.4 %copy.12 = bf16[3072,384]{1,0:T(8,128)(2,1)} copy(bf16[3072,384]{1,0:T(8,128)(2,1)S(1)} %copy-done) | data formatting | bytes 4718592
Async XLA Ops:
  119.1 3.5 %copy-start = (bf16[3072,384]{1,0:T(8,128)(2,1)S(1)}, bf16[3072,384]{1,0:T(8,128)(2,1)}, u32[]{:S(2)}) copy-start(bf16[3072,384]{1,0:T(8,128)(2,1)} %get-tuple-element.14) | copy-start | bytes 7077892

commit v2 on v0

v2 whole, which is shorter than its diff:
```python
import functools

import jax
import jax.numpy as jnp
from jax import lax
from jax.experimental import pallas as pl
from jax.experimental.pallas import tpu as pltpu
from jax.sharding import PartitionSpec as P

coeff = 0.7978845608028654
f32 = jnp.float32
bf16 = jnp.bfloat16
R, L = 0, 1
SEND_SEMS = 64
RECV_SEMS = 153

Z_REL = (0, 1, -1, 2, -2, 3, -3, 4)
GATHER_SRC = {R: (0, 2, 4, 6), L: (0, 1, 3, 5)}
GATHER_DST = {R: (2, 4, 6, 7), L: (1, 3, 5, 7)}
GROUPS = {1: (0, 3), 2: (3, 5), 3: (5, 7), 4: (7, 8)}
SUM_SRC = {R: (7, 5, 3, 1), L: (7, 6, 4, 2)}
SUM_DST = {R: (5, 3, 1, 0), L: (6, 4, 2, 0)}
X_FAR = ((0, 3), (3, 7), (7, 8))
D_FAR = ((5, 6), (6, 8))
Y_FIRST = ((1, 0), (2, 0), (1, 1), (2, 1))
CHUNKS = ((0, 0, 256), (1, 0, 256), (2, 0, 256), (3, 0, 256))
WIDE = 4
BUFS = ("PB", "RL", "FN", "AGB", "IGP", "CR", "ZR", "YF")


def gelu_pair(pre, back):
    inner = coeff * (pre + 0.044715 * pre * pre * pre)
    tanh_val = jnp.tanh(inner)
    act = 0.5 * pre * (1.0 + tanh_val)
    slope = 0.5 * (1.0 + tanh_val) + 0.5 * pre * (1.0 - tanh_val * tanh_val) * coeff * (
        1.0 + 3.0 * 0.044715 * pre * pre
    )
    return act, back * slope


class Plan:
    def __init__(self, k):
        self.k = k
        self.tasks = {}
        self.groups = {}
        self.regions = {}
        self.gather()
        self.middle()
        self.input_grad()
        self.weight_grads()

    def group(self, name, copies, region):
        self.groups.update({copy: name for copy in copies})
        self.regions[name] = region

    def task(self, name, needs=(), after=(), do=None, sends=()):
        assert name not in self.tasks
        self.tasks[name] = (tuple(needs), tuple(after), do, tuple(sends))

    def gather(self):
        k = self.k
        last = {("X", 0): (4, 3), ("D", 0): (3, 4), ("D", 1): (4, 3), ("D", 2): (3, 4), ("D", 3): (2, 2)}

        def hop(nm, sec, h, d):
            link = ("z", d)

            def refs():
                b = getattr(k, nm)
                src = b.at[sec, GATHER_SRC[d][h - 1], 0]
                if sec == 0 and h == 1:
                    src = k.x_in if nm == "X" else k.d_in
                return src, b.at[sec, GATHER_DST[d][h - 1], 0]

            return (f"{nm}{sec}z{h}{d}", link, 1, refs)

        def move(name, link, nm, sec, to, lo, hi, half=(0, 0)):
            def refs():
                b = getattr(k, nm)
                return b.at[sec, lo:hi, half[0]], b.at[to, lo:hi, half[1]]

            n = (hi - lo) * (2 if isinstance(sec, slice) else 1)
            return (name, link, n, refs)

        def hand(nm, sec, tag, lo, hi):
            return move(f"{nm}{sec}c{tag}", ("p", 0), nm, sec, sec, lo, hi, (0, 1))

        self.task(
            "go",
            sends=[hop(nm, 0, 1, d) for nm in "XD" for d in (R, L)]
            + [
                ("DyR", ("y", R), 1, lambda: (k.d_in, k.D.at[2, 0, 0])),
                ("DyL", ("y", L), 1, lambda: (k.d_in, k.D.at[1, 0, 0])),
            ],
        )
        self.task("own", after=["go"], do=lambda: k.own_wait())
        for j in range(2):
            self.task(f"t{j}", after=["own"], do=lambda j=j: k.transpose(j))
        self.task("D1s", ["DyL"], ["own"], sends=[hop("D", 1, 1, d) for d in (R, L)])
        self.task(
            "D2s",
            ["DyR"],
            ["own"],
            sends=[
                ("Dy2", ("y", R), 1, lambda: (k.D.at[2, 0, 0], k.D.at[3, 0, 0])),
                *(hop("D", 2, 1, d) for d in (R, L)),
            ],
        )
        self.task("D3s", ["Dy2"], ["own"], sends=[hop("D", 3, 1, d) for d in (R, L)])
        for (nm, sec), hops in last.items():
            for d in (R, L):
                for h in range(1, hops[d] + 1):
                    more = [hop(nm, sec, h + 1, d)] if h < hops[d] else []
                    self.task(f"{nm}{sec}z{h}{d}", [f"{nm}{sec}z{h}{d}"], ["own"], sends=more)
            for h, (lo, hi) in GROUPS.items():
                got = [f"{nm}{sec}z{h}{d}" for d in (R, L) if h <= hops[d]]
                if not got:
                    continue
                sends = []
                if nm == "X":
                    sends.append(move(f"Xy{h}{R}", ("y", R), "X", 0, 2, lo, hi))
                    sends.append(move(f"Xy{h}{L}", ("y", L), "X", 0, 1, lo, hi))
                sends.append(hand(nm, sec, h, lo, hi))
                if nm == "D" and sec == 2 and h == 3:
                    sends.insert(0, move("Df0", ("y", R), "D", 2, 3, *D_FAR[0]))
                if nm == "D" and sec == 1 and h == 4:
                    got.append("D1g3")
                    sends.insert(0, move("Df1", ("y", L), "D", 1, 3, *D_FAR[1]))
                if nm == "D" and sec > 0:
                    got.append(f"D{sec}s")
                self.task(f"{nm}{sec}g{h}", after=got, sends=sends)
        for h, (lo, hi) in GROUPS.items():
            sends = []
            if h == 1:
                sends.append(move("Xf0", ("y", R), "X", 2, 3, *X_FAR[0]))
            if h == 3:
                sends.append(move("Xf1", ("y", L), "X", 1, 3, *X_FAR[1]))
            if h == 4:
                sends.append(move("Xf2", ("y", R), "X", 2, 3, *X_FAR[2]))
            sends.append(move(f"Xyc{h}", ("p", 0), "X", slice(1, 3), slice(1, 3), lo, hi, (0, 1)))
            prior = ["own"] if h == 1 else [f"Xy{h - 1}"]
            self.task(f"Xy{h}", [f"Xy{h}{R}", f"Xy{h}{L}"], prior, sends=sends)
        for nm, far in (("X", X_FAR), ("D", D_FAR)):
            for i, (lo, hi) in enumerate(far):
                self.task(
                    f"{nm}f{i}", [f"{nm}f{i}"], ["own"], sends=[hand(nm, 3, f"f{i}", lo, hi)]
                )
        self.has = {
            (nm, sec): [
                *(f"{nm}{sec}g{h}" for h in GROUPS if f"{nm}{sec}g{h}" in self.tasks),
                *((f"{nm}f{i}" for i in range(len(far))) if sec == 3 else ()),
                *((f"Xy{h}" for h in GROUPS) if nm == "X" and sec in (1, 2) else ()),
            ]
            for nm, far in (("X", X_FAR), ("D", D_FAR))
            for sec in range(4)
        }
        self.hands = {}
        for (nm, sec), names in self.has.items():
            copies = []
            for n in names:
                copies += [c[0] for c in self.tasks[n][3] if c[1][0] == "p"]
            self.hands[nm, sec] = copies
            at = slice(1, 3) if nm == "X" and sec in (1, 2) else sec
            self.group(f"{nm}{at}", copies, lambda nm=nm, at=at: getattr(k, nm).at[at, :, 1])

    def middle(self):
        k = self.k
        for s, (sec, _, width) in enumerate(CHUNKS):
            w = width / 256
            for j, nm, d, e in ((0, "X", R, L), (1, "D", L, R)):
                self.task(
                    f"m{s}{j}",
                    self.hands[nm, sec],
                    [*self.has[nm, sec], f"t{j}"],
                    lambda s=s, j=j: k.partial(s, j),
                    [
                        (f"r{s}{d}", ("x", d), w / 2,
                         lambda s=s, j=j: (k.at("PB", s).at[j, k.rows("far")], k.at("RL", s).at[j])),
                        (f"f{s}{j}{e}", ("x", e), w / 2,
                         lambda s=s, j=j, e=e: (k.at("PB", s).at[j, k.rows(e)], k.at("FN", s).at[e, j])),
                    ],
                )
                self.task(
                    f"l{s}{j}",
                    [f"r{s}{d}"],
                    [f"m{s}{j}"],
                    lambda s=s, j=j, d=d: k.relay(s, j, d),
                    [
                        (f"f{s}{j}{d}", ("x", d), w / 2,
                         lambda s=s, j=j, d=d: (k.at("PB", s).at[j, k.rows(d)], k.at("FN", s).at[d, j])),
                    ],
                )
            self.group(
                f"f{s}",
                [f"f{s}{j}{d}" for j in range(2) for d in (R, L)],
                lambda s=s: k.at("FN", s),
            )
            for j in range(2):
                self.group(
                    f"h{s}{j}",
                    [f"h{s}{j}{R}", f"h{s}{j}{L}"],
                    lambda s=s, j=j: k.at("AGB", s).at[j, k.rows("far")],
                )

            def mine(s=s, j=1):
                return (k.at("AGB", s).at[j, k.rows("own")],) * 2

            self.task(
                f"g{s}",
                [f"f{s}{j}{d}" for j in range(2) for d in (R, L)],
                [f"m{s}0", f"m{s}1"],
                lambda s=s: k.gelu(s),
                [(f"a{s}1{d}", ("x", d), w / 2, mine) for d in (R, L)],
            )
            self.task(
                f"u{s}",
                (),
                [f"g{s}"],
                None,
                [(f"a{s}0{d}", ("x", d), w / 2, lambda s=s: mine(s, 0)) for d in (R, L)],
            )
            for j, before in ((1, f"g{s}"), (0, f"u{s}")):
                for d, e in ((R, L), (L, R)):
                    self.task(
                        f"h{s}{j}{d}",
                        [f"a{s}{j}{d}"],
                        [before],
                        None,
                        [
                            (f"h{s}{j}{d}", ("x", d), w / 4,
                             lambda s=s, j=j, d=d, e=e: (k.at("AGB", s).at[j, k.rows(e, d)],) * 2),
                        ],
                    )

    def input_grad(self):
        k = self.k

        def first(s, q, d):
            return 0 if (s + q) % 2 == d else 1

        def start_slot(s, q, d):
            return SUM_SRC[d][first(s, q, d)]

        def half(q):
            return slice(96 * q, 96 * q + 96)

        def zsend(s, q, d, j):
            return (f"S{s}{q}{d}{j}", ("z", d), CHUNKS[s][2] / 512,
                    lambda: (k.at("IGP", s).at[SUM_SRC[d][j], 0, half(q)], k.at("ZR", s).at[d, j, half(q)]))

        def starts(s, q, p):
            return [zsend(s, q, d, first(s, q, d)) for d in (R, L) if start_slot(s, q, d) // 2 == p]

        late = {q for _, q in Y_FIRST}
        for s in range(len(CHUNKS)):
            for p in (3, 2, 1, 0):
                pair = slice(2 * p, 2 * p + 2)
                self.task(
                    f"i{s}{p}",
                    [f"a{s}1{R}", f"a{s}1{L}", f"h{s}1{R}", f"h{s}1{L}"],
                    [f"h{s}1{R}", f"h{s}1{L}"],
                    lambda s=s, p=p: k.ig_part(s, p),
                    [(f"C{s}{p}", ("p", 0), CHUNKS[s][2] / 128,
                      lambda s=s, pair=pair: (k.at("IGP", s).at[pair, 1], k.at("CR", s).at[pair]))],
                )
                sends = []
                for q in range(2):
                    if (s, q) in Y_FIRST:
                        sends.append((f"A{s}{q}{p}", ("y", s - 1), 1,
                                      lambda s=s, q=q, pair=pair: (k.at("IGP", s).at[pair, 0, half(q)],
                                                                   k.YA.at[s - 1, pair, half(q)])))
                    elif s > 0 or q not in late:
                        sends += starts(s, q, p)
                self.task(
                    f"c{s}{p}", [f"C{s}{p}"], [f"i{s}{p}"], lambda s=s, p=p: k.core_sum(s, p), sends
                )
                for q in sorted(late):
                    if s == 0:
                        froms = [t for t in (1, 2) if (t, q) in Y_FIRST]
                        self.task(
                            f"y{q}{p}",
                            [f"A{t}{q}{p}" for t in froms],
                            [f"c0{p}"] + [f"c{t}{p}" for t in froms],
                            lambda p=p, q=q, froms=froms: k.y_sum(p, half(q), froms),
                            starts(0, q, p),
                        )
        finals = {0: [], 1: []}
        for s in range(len(CHUNKS)):
            for q in range(2):
                if (s, q) in Y_FIRST:
                    continue

                def ready(slot, s=s, q=q):
                    return f"y{q}{slot // 2}" if s == 0 and q in late else f"c{s}{slot // 2}"

                for d in (R, L):
                    for j in range(first(s, q, d), 3):
                        self.task(
                            f"z{s}{q}{d}{j}",
                            [f"S{s}{q}{d}{j}"],
                            [ready(SUM_DST[d][j]), ready(start_slot(s, q, d))],
                            lambda s=s, q=q, d=d, j=j: k.z_sum(s, half(q), d, j),
                            [zsend(s, q, d, j + 1)],
                        )
                sends = []
                if s > 0:
                    link = ("y", (R, L, "far")[CHUNKS[s][0] - 1])
                    finals[q].append(f"F{s}{q}")
                    sends = [(f"F{s}{q}", link, CHUNKS[s][2] / 512,
                              lambda s=s, q=q: (k.at("IGP", s).at[0, 0, half(q)], k.at("YF", s).at[half(q)]))]
                self.task(
                    f"e{s}{q}",
                    [f"S{s}{q}{d}3" for d in (R, L)],
                    [f"z{s}{q}{d}2" for d in (R, L)] + [ready(0)],
                    lambda s=s, q=q: k.z_end(s, half(q)),
                    sends,
                )
        for q in range(2):
            froms = [int(n[1]) for n in finals[q]]
            self.task(
                f"end{q}",
                finals[q],
                [f"e0{q}"] + [f"e{t}{q}" for t in froms],
                lambda q=q, froms=froms: k.end(half(q), froms),
            )

    def weight_grads(self):
        k = self.k
        for s in range(len(CHUNKS)):
            for j in range(2):
                self.task(
                    f"v{s}{j}",
                    [f"a{s}{j}{R}", f"a{s}{j}{L}", f"h{s}{j}{R}", f"h{s}{j}{L}"],
                    [f"h{s}{j}{R}", f"h{s}{j}{L}"],
                    lambda s=s, j=j: k.turn_act(s, j),
                )
        for which, j in ((0, 1), (1, 0)):
            for slot in range(8):
                self.task(
                    f"w{which}{slot}",
                    (),
                    [f"v{s}{j}" for s in range(len(CHUNKS))] + ["t1"],
                    lambda which=which, slot=slot: k.weight_grad(which, slot),
                )


class Device:
    def __init__(self, **refs):
        self.__dict__.update(refs)

    def at(self, name, chunk):
        i = BUFS.index(name)
        return self.wide[i].at[chunk] if chunk < WIDE else self.narrow[i].at[chunk - WIDE]

    def block_rows(self, slot, other):
        row = turn(self.z, Z_REL[slot], self.n_z) * 2 + (1 - self.core if other else self.core)
        return pl.ds(pl.multiple_of(row * 192, 192), 192)

    def load(self):
        self.own = [
            pltpu.make_async_copy(a, b.at[0, 0, 0], self.local_sems.at[i])
            for i, (a, b) in enumerate(((self.x_in, self.X), (self.d_in, self.D)))
        ]
        for copy in self.own:
            copy.start()
        for i, src in enumerate((self.wu_in, self.wd_in)):
            for slot in range(8):
                for other in range(2):
                    rows = pl.ds((slot * 2 + other) * 192, 192)
                    dst = self.WU.at[slot, other] if i == 0 else self.gd_out.at[rows]
                    pltpu.make_async_copy(
                        src.at[self.block_rows(slot, other)], dst, self.local_sems.at[2 + i]
                    ).start()

    def own_wait(self):
        for copy in self.own:
            copy.wait()

    def transpose(self, j):
        src, dst = ((self.WU, self.UT), (self.gd_out, self.DT))[j]
        pltpu.make_async_copy(src, src, self.local_sems.at[2 + j]).wait()

        @pl.loop(0, 4)
        def _(p):
            if j == 0:
                dst[p] = src[pl.ds(p * 2, 2)].reshape(768, 384).T
            else:
                dst[p] = src[pl.ds(pl.multiple_of(p * 768, 768), 768)].T

    def rows(self, which, part=None):
        by = {R: 1, L: -1, "far": 2, "own": 0}[which]
        at = turn(self.c, by, self.n_col) * 96
        if part is None:
            return pl.ds(pl.multiple_of(at, 96), 96)
        return pl.ds(pl.multiple_of(at + 48 * part, 48), 48)

    def partial(self, s, j):
        b, w = ((self.X, self.UT), (self.D, self.DT))[j]
        sec, lane, width = CHUNKS[s]
        acc = jnp.zeros((384, width), f32)
        for p in range(4):
            tokens = b[sec, 2 * p : 2 * p + 2, :, :, lane : lane + width].reshape(768, width)
            acc += jnp.dot(w[p], tokens, preferred_element_type=f32)
        self.at("PB", s)[j] = acc.astype(bf16)

    def relay(self, s, j, d):
        rows = self.rows(d)
        self.at("PB", s)[j, rows] = (
            self.at("PB", s)[j, rows].astype(f32) + self.at("RL", s)[j].astype(f32)
        ).astype(bf16)

    def gelu(self, s):
        rows = self.rows("own")
        pre, back = (
            self.at("PB", s)[j, rows].astype(f32)
            + self.at("FN", s)[0, j].astype(f32)
            + self.at("FN", s)[1, j].astype(f32)
            for j in range(2)
        )
        act, grad = gelu_pair(pre, back)
        self.at("AGB", s)[0, rows] = act.astype(bf16)
        self.at("AGB", s)[1, rows] = grad.astype(bf16)

    def ig_part(self, s, p):
        w = self.WU[2 * p : 2 * p + 2].reshape(768, 384)
        g = jnp.dot(w, self.at("AGB", s)[1], preferred_element_type=f32)
        self.at("IGP", s)[2 * p : 2 * p + 2] = g.astype(bf16).reshape(2, 2, 192, CHUNKS[s][2])

    def core_sum(self, s, p):
        pair = slice(2 * p, 2 * p + 2)
        self.at("IGP", s)[pair, 0] = (
            self.at("IGP", s)[pair, 0].astype(f32) + self.at("CR", s)[pair].astype(f32)
        ).astype(bf16)

    def y_sum(self, p, rows, froms):
        pair = slice(2 * p, 2 * p + 2)
        total = self.at("IGP", 0)[pair, 0, rows].astype(f32)
        for t in froms:
            total += self.YA[t - 1, pair, rows].astype(f32)
        self.at("IGP", 0)[pair, 0, rows] = total.astype(bf16)

    def z_sum(self, s, rows, d, j):
        slot = SUM_DST[d][j]
        self.at("IGP", s)[slot, 0, rows] = (
            self.at("IGP", s)[slot, 0, rows].astype(f32) + self.at("ZR", s)[d, j, rows].astype(f32)
        ).astype(bf16)

    def z_end(self, s, rows):
        total = (
            self.at("IGP", s)[0, 0, rows].astype(f32)
            + self.at("ZR", s)[0, 3, rows].astype(f32)
            + self.at("ZR", s)[1, 3, rows].astype(f32)
        )
        if s == 0:
            self.ig_out[rows] = total
        else:
            self.at("IGP", s)[0, 0, rows] = total.astype(bf16)

    def end(self, rows, froms):
        for t in froms:
            lanes = slice(CHUNKS[t][1], CHUNKS[t][1] + CHUNKS[t][2])
            self.ig_out[rows, lanes] = self.ig_out[rows, lanes] + self.at("YF", t)[rows].astype(f32)

    def turn_act(self, s, j):
        sec, lane, width = CHUNKS[s]
        self.AT[j, sec, lane : lane + width] = self.at("AGB", s)[j].T

    def weight_grad(self, which, slot):
        b, j, out = ((self.X, 1, self.gu_out), (self.D, 0, self.gd_out))[which]
        acc = jnp.zeros((384, 384), f32)
        for s in range(4):
            acc += jnp.dot(
                b[s, slot].reshape(384, 256), self.AT[j, s], preferred_element_type=f32
            )
        acc = acc.astype(bf16)
        out[self.block_rows(slot, 0), :] = acc[:192]
        out[self.block_rows(slot, 1), :] = acc[192:]


def turn(i, by, n):
    return lax.rem(i + (by + n), n)


ORDER = (
    0, 1, 3, 7, 11, 14, 18, 21, 25, 8, 12, 15, 4, 22, 19, 2, 13, 9, 16, 29, 5, 23, 33, 36, 26,
    20, 10, 17, 27, 57, 43, 30, 24, 28, 58, 59, 40, 66, 34, 47, 68, 31, 60, 37, 44, 41, 48, 6,
    67, 69, 35, 76, 38, 32, 39, 45, 86, 42, 49, 78, 62, 53, 70, 51, 55, 46, 50, 63, 61, 71, 77,
    79, 65, 88, 54, 64, 72, 73, 52, 56, 96, 87, 98, 89, 80, 173, 97, 110, 74, 99, 90, 82, 106,
    83, 118, 100, 114, 93, 92, 101, 122, 124, 175, 126, 111, 102, 103, 91, 81, 130, 134, 132,
    177, 123, 131, 138, 104, 140, 75, 119, 107, 95, 125, 139, 105, 179, 182, 133, 141, 136, 135,
    84, 108, 142, 127, 160, 164, 85, 109, 178, 180, 115, 167, 143, 172, 158, 137, 181, 112, 94,
    146, 128, 161, 165, 144, 154, 149, 113, 174, 185, 129, 145, 159, 168, 176, 116, 147, 184,
    162, 191, 166, 155, 189, 117, 152, 150, 193, 186, 195, 163, 120, 148, 169, 194, 156, 121,
    153, 183, 187, 190, 192, 188, 151, 170, 157, 171,
)


def kernel(
    x_in, d_in, wu_in, wd_in,
    ig_out, gu_out, gd_out,
    X, D, WU, UT, DT, AT, YA,
    send_sems, recv_sems, local_sems,
    *chunk_bufs,
):
    refs = dict(locals())
    n_sec, n_row, n_col = (lax.axis_size(a) for a in ("section", "row", "col"))
    n_z = n_row // 2
    s, r, c = (lax.axis_index(a) for a in ("section", "row", "col"))
    z, core = r // 2, r % 2
    device_of = {("p", 0): {"row": z * 2 + (1 - core)}, ("y", "far"): {"section": turn(s, 2, n_sec)}}
    for d, by in ((R, 1), (L, -1)):
        device_of["z", d] = {"row": turn(z, by, n_z) * 2 + core}
        device_of["y", d] = {"section": turn(s, by, n_sec)}
        device_of["x", d] = {"col": turn(c, by, n_col)}

    barrier = pltpu.get_barrier_semaphore()
    for dev in device_of.values():
        pl.semaphore_signal(barrier, inc=1, device_id=dev, device_id_type=pl.DeviceIdType.MESH)
    here = Device(**refs, wide=chunk_bufs[: len(BUFS)], narrow=chunk_bufs[len(BUFS) :], z=z, core=core, c=c, n_z=n_z, n_col=n_col)
    here.load()
    pl.semaphore_wait(barrier, len(device_of))

    plan = Plan(here)
    tasks, groups = plan.tasks, plan.groups
    started, descriptors, arrived, done, recv_of = {}, [], set(), set(), {}
    names = list(tasks)
    assert sorted(ORDER) == list(range(len(names)))
    for name in (names[i] for i in ORDER):
        needs, after, do, sends = tasks[name]
        assert done.issuperset(after)
        for copy in needs:
            key = groups.get(copy, copy)
            if key not in arrived:
                arrived.add(key)
                if key in plan.regions:
                    region = plan.regions[key]()
                    pltpu.make_async_copy(region, region, recv_sems.at[recv_of[key]]).wait()
                else:
                    started[copy].wait_recv()
        if do is not None:
            do()
        for copy, link, _, of in sends:
            src, dst = of()
            i = len(descriptors)
            if i >= SEND_SEMS:
                descriptors[i - SEND_SEMS].wait_send()
            started[copy] = pltpu.make_async_remote_copy(
                src_ref=src,
                dst_ref=dst,
                send_sem=send_sems.at[i % SEND_SEMS],
                recv_sem=recv_sems.at[recv_of.setdefault(groups.get(copy, copy), len(recv_of))],
                device_id=device_of[link],
                device_id_type=pl.DeviceIdType.MESH,
            )
            started[copy].start()
            descriptors.append(started[copy])
        done.add(name)
    assert arrived == set(recv_of) and len(recv_of) <= RECV_SEMS
    for copy in descriptors[-SEND_SEMS:]:
        copy.wait_send()


def chunk_buffers(n, width):
    shapes = (
        (2, 384),
        (2, 96),
        (2, 2, 96),
        (2, 384),
        (8, 2, 192),
        (8, 192),
        (2, 4, 192),
        (192,),
    )
    return [pltpu.VMEM((n, *shape, width), bf16) for shape in shapes]


def on_device(inputs, out_grad, w_up, w_down):
    any_spec = pl.BlockSpec(memory_space=pl.ANY)
    ig_t, gu, gd = pl.pallas_call(
        kernel,
        out_shape=(
            pltpu.VMEM((192, 256), f32),
            pltpu.VMEM((3072, 384), bf16),
            pltpu.VMEM((3072, 384), bf16),
        ),
        in_specs=[any_spec] * 4,
        out_specs=(pl.BlockSpec(memory_space=pltpu.VMEM),) * 3,
        scratch_shapes=[
            pltpu.VMEM((4, 8, 2, 192, 256), bf16),
            pltpu.VMEM((4, 8, 2, 192, 256), bf16),
            pltpu.VMEM((8, 2, 192, 384), bf16),
            pltpu.VMEM((4, 384, 768), bf16),
            pltpu.VMEM((4, 384, 768), bf16),
            pltpu.VMEM((2, 4, 256, 384), bf16),
            pltpu.VMEM((2, 8, 192, 256), bf16),
            pltpu.SemaphoreType.DMA((SEND_SEMS,)),
            pltpu.SemaphoreType.DMA((RECV_SEMS,)),
            pltpu.SemaphoreType.DMA((4,)),
            *chunk_buffers(WIDE, 256),
            *(chunk_buffers(len(CHUNKS) - WIDE, 128) if len(CHUNKS) > WIDE else ()),
        ],
        compiler_params=pltpu.CompilerParams(
            collective_id=0, has_side_effects=True, vmem_limit_bytes=52 * 2**20
        ),
        cost_estimate=pl.CostEstimate(
            flops=5 * 2 * 1024 * 3072 * 384, bytes_accessed=10_000_000, transcendentals=98304
        ),
        name="ffn_backward",
    )(inputs.T, out_grad.T, w_up, w_down)
    return ig_t.T, gu, gd


def solution(mesh):
    return jax.shard_map(
        on_device,
        mesh=mesh,
        in_specs=(
            P("section", ("col", "row")),
            P("section", ("col", "row")),
            P("col", ("section", "row")),
            P("col", ("section", "row")),
        ),
        out_specs=(
            P("section", ("col", "row")),
            P("col", ("section", "row")),
            P("col", ("section", "row")),
        ),
        check_vma=False,
    )
```

time: 756 us -> 95.3 us (0.13)
  waiting for transfers between devices: 349 us -> 0 us
  local copies, waits for them, and re-layouts: 319 us -> 3.49 us
  Pallas kernels: 0 us -> 90.7 us
  matrix products: 40.7 us -> 0 us
  blocking collectives: 28.7 us -> 0 us
  between operations: 14.2 us -> 0.64 us
    gather x384 -> x0, local copies, waits for them, and re-layouts: 299 us -> none
    all_gather x4 -> x0, waiting for transfers between devices: 224 us -> none  [the longest x1 72.8 us: on_device(): lax.all_gather(dy_wide, 'section', axis=0, tiled=True)]
    reduce_scatter x3 -> x0, waiting for transfers between devices: 124 us -> none  [the longest x1 124 us: on_device(): lax.psum_scatter(jax.vmap(one_target)(targets).reshape(lax.axis_size(('se...]
    pallas_call x0 -> x1, Pallas kernels: none -> 90.7 us  [on_device(): pl.pallas_call(kernel, out_shape=(pltpu.VMEM((192, 256), f32), pltpu.VMEM...]
    dot_general x5 -> x0, matrix products: 40.7 us -> none  [the longest x2 14.2 us: token_sum(): lax.dot_general(left, right, (((0,), (0,)), ((), ())), preferred_element_...]
    all_gather x2 -> x0, blocking collectives: 28.7 us -> none  [the longest x1 14.5 us: on_device(): lax.all_gather(act, 'col', axis=0, tiled=True)]
    reshape x1 -> x0, local copies, waits for them, and re-layouts: 10.7 us -> none  [on_device(): jax.vmap(one_target)(targets)]
  transfers between devices with their start and end apart: 7 -> 0, of which waited for: 5 -> 0; matrix products, arithmetic and copies ran while one was open for 28% -> 0% of each run, Pallas kernels for 0% -> 0%
where the time goes in v2:
time: 95.3 us; the launch traced here: 94.8 us
  Pallas kernels  90.7 us (95%)
  local copies, waits for them, and re-layouts  3.49 us (4%)
    pallas_call x1, Pallas kernels, on_device(): pl.pallas_call(kernel, out_shape=(pltpu.VMEM((192, 256), f32), pltpu.VMEM...  90.7 us
    unnamed x3, local copies, waits for them, and re-layouts  3.49 us

profile of v2, /device:TPU:2, one launch (start us, length us, event | category | flops | bytes accessed | tf_op | source)
XLA Modules:
  0.0 94.8 jit_solution(16385706482369766017)
XLA Ops:
  0.6 90.7 %ffn_backward.1 = (f32[192,256]{1,0:T(8,128)S(1)}, bf16[3072,384]{1,0:T(8,128)(2,1)S(1)}, bf16[3072,384]{1,0:T(8,128)(2,1)S(1)}) custom-call(bf16[192,256]{1,0:T(8,128)(2,1)} %bitcast.4, bf16[192,256]{1,0:T(8,128)(2,1)} %bitcast.5, bf16[3072,384]{1,0:T(8,128)(2,1)} %wu_in.1, bf16[3072,384]{1,0:T(8,128)(2,1)} %wd_in.1), custom_call_target="tpu_custom_call" | custom-call | flops 12079595520 | bytes 10000000 | tf_op jit(solution)/shard_map/ffn_backward/pallas_call | solution.py:578
  91.4 0.7 copy.10
  92.0 1.4 %copy.11 = bf16[3072,384]{1,0:T(8,128)(2,1)} copy(bf16[3072,384]{1,0:T(8,128)(2,1)S(1)} %get-tuple-element.10) | data formatting | bytes 4718592
  93.4 1.4 %copy.12 = bf16[3072,384]{1,0:T(8,128)(2,1)} copy(bf16[3072,384]{1,0:T(8,128)(2,1)S(1)} %get-tuple-element.11) | data formatting | bytes 4718592

commit v3 on v2

--- a/solution.py
+++ b/solution.py
@@ -11,7 +11,7 @@
 f32 = jnp.float32
 bf16 = jnp.bfloat16
 R, L = 0, 1
-SEND_SEMS = 64
+SEND_SEMS = 48
 RECV_SEMS = 153
 
 Z_REL = (0, 1, -1, 2, -2, 3, -3, 4)
@@ -25,6 +25,7 @@
 Y_FIRST = ((1, 0), (2, 0), (1, 1), (2, 1))
 CHUNKS = ((0, 0, 256), (1, 0, 256), (2, 0, 256), (3, 0, 256))
 WIDE = 4
+DIRECT = (0, 1, 2, 3)
 BUFS = ("PB", "RL", "FN", "AGB", "IGP", "CR", "ZR", "YF")
 
 
@@ -195,6 +196,8 @@
                 lambda s=s: k.at("FN", s),
             )
             for j in range(2):
+                if j == 1 and s in DIRECT:
+                    continue
                 self.group(
                     f"h{s}{j}",
                     [f"h{s}{j}{R}", f"h{s}{j}{L}"],
@@ -209,7 +212,8 @@
                 [f"f{s}{j}{d}" for j in range(2) for d in (R, L)],
                 [f"m{s}0", f"m{s}1"],
                 lambda s=s: k.gelu(s),
-                [(f"a{s}1{d}", ("x", d), w / 2, mine) for d in (R, L)],
+                [(f"a{s}1{d}", ("x", d), w / 2, mine)
+                 for d in ((*(("far",) if s in DIRECT else ()), R, L))],
             )
             self.task(
                 f"u{s}",
@@ -220,6 +224,8 @@
             )
             for j, before in ((1, f"g{s}"), (0, f"u{s}")):
                 for d, e in ((R, L), (L, R)):
+                    if j == 1 and s in DIRECT:
+                        continue
                     self.task(
                         f"h{s}{j}{d}",
                         [f"a{s}{j}{d}"],
@@ -231,6 +237,13 @@
                         ],
                     )
 
+    def spread(self, s, j):
+        copies = [f"a{s}{j}{d}" for d in (R, L)]
+        if j == 1 and s in DIRECT:
+            return [*copies, f"a{s}1far"], [f"g{s}"]
+        relays = [f"h{s}{j}{d}" for d in (R, L)]
+        return copies + relays, relays
+
     def input_grad(self):
         k = self.k
 
@@ -256,8 +269,7 @@
                 pair = slice(2 * p, 2 * p + 2)
                 self.task(
                     f"i{s}{p}",
-                    [f"a{s}1{R}", f"a{s}1{L}", f"h{s}1{R}", f"h{s}1{L}"],
-                    [f"h{s}1{R}", f"h{s}1{L}"],
+                    *self.spread(s, 1),
                     lambda s=s, p=p: k.ig_part(s, p),
                     [(f"C{s}{p}", ("p", 0), CHUNKS[s][2] / 128,
                       lambda s=s, pair=pair: (k.at("IGP", s).at[pair, 1], k.at("CR", s).at[pair]))],
@@ -329,8 +341,7 @@
             for j in range(2):
                 self.task(
                     f"v{s}{j}",
-                    [f"a{s}{j}{R}", f"a{s}{j}{L}", f"h{s}{j}{R}", f"h{s}{j}{L}"],
-                    [f"h{s}{j}{R}", f"h{s}{j}{L}"],
+                    *self.spread(s, j),
                     lambda s=s, j=j: k.turn_act(s, j),
                 )
         for which, j in ((0, 1), (1, 0)):
@@ -481,16 +492,16 @@
 
 
 ORDER = (
-    0, 1, 3, 7, 11, 14, 18, 21, 25, 8, 12, 15, 4, 22, 19, 2, 13, 9, 16, 29, 5, 23, 33, 36, 26,
-    20, 10, 17, 27, 57, 43, 30, 24, 28, 58, 59, 40, 66, 34, 47, 68, 31, 60, 37, 44, 41, 48, 6,
-    67, 69, 35, 76, 38, 32, 39, 45, 86, 42, 49, 78, 62, 53, 70, 51, 55, 46, 50, 63, 61, 71, 77,
-    79, 65, 88, 54, 64, 72, 73, 52, 56, 96, 87, 98, 89, 80, 173, 97, 110, 74, 99, 90, 82, 106,
-    83, 118, 100, 114, 93, 92, 101, 122, 124, 175, 126, 111, 102, 103, 91, 81, 130, 134, 132,
-    177, 123, 131, 138, 104, 140, 75, 119, 107, 95, 125, 139, 105, 179, 182, 133, 141, 136, 135,
-    84, 108, 142, 127, 160, 164, 85, 109, 178, 180, 115, 167, 143, 172, 158, 137, 181, 112, 94,
-    146, 128, 161, 165, 144, 154, 149, 113, 174, 185, 129, 145, 159, 168, 176, 116, 147, 184,
-    162, 191, 166, 155, 189, 117, 152, 150, 193, 186, 195, 163, 120, 148, 169, 194, 156, 121,
-    153, 183, 187, 190, 192, 188, 151, 170, 157, 171,
+    0, 1, 7, 11, 14, 18, 21, 25, 8, 12, 15, 4, 9, 22, 13, 16, 19, 2, 29, 26, 5, 23, 10, 17, 33,
+    57, 58, 3, 43, 20, 27, 66, 30, 24, 28, 59, 40, 34, 37, 36, 68, 31, 60, 47, 67, 44, 6, 82,
+    41, 69, 35, 38, 74, 32, 39, 45, 48, 61, 76, 51, 53, 55, 70, 42, 49, 75, 63, 46, 50, 62, 77,
+    65, 84, 54, 52, 56, 83, 64, 90, 92, 98, 85, 78, 110, 106, 91, 102, 93, 165, 99, 86, 103,
+    111, 167, 107, 116, 94, 118, 114, 71, 95, 79, 122, 126, 124, 115, 87, 123, 117, 130, 132,
+    125, 136, 131, 73, 72, 171, 134, 133, 119, 128, 100, 169, 177, 127, 97, 152, 156, 101, 80,
+    96, 120, 159, 135, 150, 174, 88, 89, 81, 104, 138, 141, 121, 176, 153, 157, 178, 146, 137,
+    105, 151, 172, 129, 160, 166, 108, 139, 168, 173, 170, 154, 158, 179, 147, 109, 144, 164,
+    180, 186, 175, 112, 140, 155, 142, 161, 148, 113, 145, 181, 187, 185, 184, 183, 182, 143,
+    162, 149, 163,
 )
 
 
@@ -507,6 +518,8 @@
     s, r, c = (lax.axis_index(a) for a in ("section", "row", "col"))
     z, core = r // 2, r % 2
     device_of = {("p", 0): {"row": z * 2 + (1 - core)}, ("y", "far"): {"section": turn(s, 2, n_sec)}}
+    if DIRECT:
+        device_of["x", "far"] = {"col": turn(c, 2, n_col)}
     for d, by in ((R, 1), (L, -1)):
         device_of["z", d] = {"row": turn(z, by, n_z) * 2 + core}
         device_of["y", d] = {"section": turn(s, by, n_sec)}

time: 95.3 us -> 92.5 us (0.971)
  Pallas kernels: 90.7 us -> 88.3 us
    pallas_call x1, Pallas kernels: 90.7 us -> 88.3 us  [on_device(): pl.pallas_call(kernel, out_shape=(pltpu.VMEM((192, 256), f32), pltpu.VMEM...]
where the time goes in v3:
time: 92.5 us; the launch traced here: 92.4 us
  Pallas kernels  88.3 us (95%)
  local copies, waits for them, and re-layouts  3.49 us (4%)
    pallas_call x1, Pallas kernels, on_device(): pl.pallas_call(kernel, out_shape=(pltpu.VMEM((192, 256), f32), pltpu.VMEM...  88.3 us
    unnamed x3, local copies, waits for them, and re-layouts  3.49 us

profile of v3, /device:TPU:2, one launch (start us, length us, event | category | flops | bytes accessed | tf_op | source)
XLA Modules:
  0.0 92.4 jit_solution(18242874073679497867)
XLA Ops:
  0.6 88.3 %ffn_backward.1 = (f32[192,256]{1,0:T(8,128)S(1)}, bf16[3072,384]{1,0:T(8,128)(2,1)S(1)}, bf16[3072,384]{1,0:T(8,128)(2,1)S(1)}) custom-call(bf16[192,256]{1,0:T(8,128)(2,1)} %bitcast.4, bf16[192,256]{1,0:T(8,128)(2,1)} %bitcast.5, bf16[3072,384]{1,0:T(8,128)(2,1)} %wu_in.1, bf16[3072,384]{1,0:T(8,128)(2,1)} %wd_in.1), custom_call_target="tpu_custom_call" | custom-call | flops 12079595520 | bytes 10000000 | tf_op jit(solution)/shard_map/ffn_backward/pallas_call | solution.py:591
  88.9 0.7 copy.10
  89.6 1.4 %copy.11 = bf16[3072,384]{1,0:T(8,128)(2,1)} copy(bf16[3072,384]{1,0:T(8,128)(2,1)S(1)} %get-tuple-element.10) | data formatting | bytes 4718592
  91.0 1.4 %copy.12 = bf16[3072,384]{1,0:T(8,128)(2,1)} copy(bf16[3072,384]{1,0:T(8,128)(2,1)S(1)} %get-tuple-element.11) | data formatting | bytes 4718592

commit v4 on v3

--- a/solution.py
+++ b/solution.py
@@ -12,7 +12,7 @@
 bf16 = jnp.bfloat16
 R, L = 0, 1
 SEND_SEMS = 48
-RECV_SEMS = 153
+RECV_SEMS = 78
 
 Z_REL = (0, 1, -1, 2, -2, 3, -3, 4)
 GATHER_SRC = {R: (0, 2, 4, 6), L: (0, 1, 3, 5)}
@@ -492,15 +492,15 @@
 
 
 ORDER = (
-    0, 1, 7, 11, 14, 18, 21, 25, 8, 12, 15, 4, 9, 22, 13, 16, 19, 2, 29, 26, 5, 23, 10, 17, 33,
-    57, 58, 3, 43, 20, 27, 66, 30, 24, 28, 59, 40, 34, 37, 36, 68, 31, 60, 47, 67, 44, 6, 82,
-    41, 69, 35, 38, 74, 32, 39, 45, 48, 61, 76, 51, 53, 55, 70, 42, 49, 75, 63, 46, 50, 62, 77,
-    65, 84, 54, 52, 56, 83, 64, 90, 92, 98, 85, 78, 110, 106, 91, 102, 93, 165, 99, 86, 103,
-    111, 167, 107, 116, 94, 118, 114, 71, 95, 79, 122, 126, 124, 115, 87, 123, 117, 130, 132,
-    125, 136, 131, 73, 72, 171, 134, 133, 119, 128, 100, 169, 177, 127, 97, 152, 156, 101, 80,
-    96, 120, 159, 135, 150, 174, 88, 89, 81, 104, 138, 141, 121, 176, 153, 157, 178, 146, 137,
-    105, 151, 172, 129, 160, 166, 108, 139, 168, 173, 170, 154, 158, 179, 147, 109, 144, 164,
-    180, 186, 175, 112, 140, 155, 142, 161, 148, 113, 145, 181, 187, 185, 184, 183, 182, 143,
+    0, 1, 2, 7, 11, 14, 18, 21, 8, 12, 15, 4, 22, 25, 19, 13, 9, 16, 29, 5, 26, 3, 23, 33, 36,
+    20, 27, 43, 10, 17, 57, 30, 24, 28, 58, 59, 66, 40, 47, 34, 37, 68, 31, 44, 60, 6, 35, 41,
+    48, 38, 69, 67, 82, 32, 39, 45, 74, 61, 76, 51, 53, 55, 70, 42, 49, 71, 46, 50, 83, 62, 75,
+    63, 84, 65, 77, 54, 52, 56, 64, 90, 92, 85, 78, 98, 110, 91, 93, 106, 86, 72, 111, 165, 107,
+    99, 73, 102, 120, 167, 94, 103, 114, 116, 79, 95, 122, 124, 87, 115, 118, 123, 164, 130,
+    132, 126, 125, 131, 134, 133, 117, 128, 88, 100, 81, 136, 169, 80, 135, 171, 89, 96, 156,
+    152, 127, 97, 119, 101, 150, 159, 174, 104, 138, 137, 121, 141, 176, 157, 129, 153, 179,
+    105, 146, 168, 166, 151, 178, 173, 170, 160, 108, 158, 184, 154, 139, 187, 109, 147, 144,
+    180, 172, 177, 161, 142, 112, 140, 155, 182, 148, 113, 145, 181, 175, 185, 183, 186, 143,
     162, 149, 163,
 )
 
@@ -534,7 +534,9 @@
 
     plan = Plan(here)
     tasks, groups = plan.tasks, plan.groups
-    started, descriptors, arrived, done, recv_of = {}, [], set(), set(), {}
+    started, descriptors, done, recv_of, link_of = {}, [], set(), {}, {}
+    start_at, arrived, heard = {}, {}, {}
+    last_user = []
     names = list(tasks)
     assert sorted(ORDER) == list(range(len(names)))
     for name in (names[i] for i in ORDER):
@@ -543,7 +545,9 @@
         for copy in needs:
             key = groups.get(copy, copy)
             if key not in arrived:
-                arrived.add(key)
+                arrived[key] = len(arrived) + len(descriptors)
+                for c in [c for c in started if groups.get(c, c) == key]:
+                    heard[link_of[c]] = max(heard.get(link_of[c], -1), start_at[c])
                 if key in plan.regions:
                     region = plan.regions[key]()
                     pltpu.make_async_copy(region, region, recv_sems.at[recv_of[key]]).wait()
@@ -554,20 +558,38 @@
         for copy, link, _, of in sends:
             src, dst = of()
             i = len(descriptors)
+            key = groups.get(copy, copy)
+            link_of[copy], start_at[copy] = link, len(arrived) + i
+            back = (link[0], 1 - link[1]) if link[0] in "zyx" and link[1] != "far" else link
+            if key not in recv_of:
+                again = [
+                    n
+                    for n, user in enumerate(last_user)
+                    if key == copy == groups.get(copy, copy)
+                    and link_of.get(user) == link
+                    and user in arrived
+                    and arrived[user] < heard.get(back, -1)
+                ]
+                if again:
+                    recv_of[key] = again[0]
+                    last_user[again[0]] = key
+                else:
+                    recv_of[key] = len(last_user)
+                    last_user.append(key)
             if i >= SEND_SEMS:
                 descriptors[i - SEND_SEMS].wait_send()
             started[copy] = pltpu.make_async_remote_copy(
                 src_ref=src,
                 dst_ref=dst,
                 send_sem=send_sems.at[i % SEND_SEMS],
-                recv_sem=recv_sems.at[recv_of.setdefault(groups.get(copy, copy), len(recv_of))],
+                recv_sem=recv_sems.at[recv_of[key]],
                 device_id=device_of[link],
                 device_id_type=pl.DeviceIdType.MESH,
             )
             started[copy].start()
             descriptors.append(started[copy])
         done.add(name)
-    assert arrived == set(recv_of) and len(recv_of) <= RECV_SEMS
+    assert set(arrived) == set(recv_of) and len(last_user) <= RECV_SEMS, len(last_user)
     for copy in descriptors[-SEND_SEMS:]:
         copy.wait_send()
 

time: 92.5 us -> 91.9 us (level)
  no operation moved by 1% of the time
where the time goes in v4:
time: 91.9 us; the launch traced here: 91.7 us
  Pallas kernels  87.6 us (95%)
  local copies, waits for them, and re-layouts  3.49 us (4%)
    pallas_call x1, Pallas kernels, on_device(): pl.pallas_call(kernel, out_shape=(pltpu.VMEM((192, 256), f32), pltpu.VMEM...  87.6 us
    unnamed x3, local copies, waits for them, and re-layouts  3.49 us

profile of v4, /device:TPU:2, one launch (start us, length us, event | category | flops | bytes accessed | tf_op | source)
XLA Modules:
  0.0 91.7 jit_solution(15384319539717722021)
XLA Ops:
  0.6 87.6 %ffn_backward.1 = (f32[192,256]{1,0:T(8,128)S(1)}, bf16[3072,384]{1,0:T(8,128)(2,1)S(1)}, bf16[3072,384]{1,0:T(8,128)(2,1)S(1)}) custom-call(bf16[192,256]{1,0:T(8,128)(2,1)} %bitcast.4, bf16[192,256]{1,0:T(8,128)(2,1)} %bitcast.5, bf16[3072,384]{1,0:T(8,128)(2,1)} %wu_in.1, bf16[3072,384]{1,0:T(8,128)(2,1)} %wd_in.1), custom_call_target="tpu_custom_call" | custom-call | flops 12079595520 | bytes 10000000 | tf_op jit(solution)/shard_map/ffn_backward/pallas_call | solution.py:613
  88.2 0.7 copy.10
  88.9 1.4 %copy.11 = bf16[3072,384]{1,0:T(8,128)(2,1)} copy(bf16[3072,384]{1,0:T(8,128)(2,1)S(1)} %get-tuple-element.10) | data formatting | bytes 4718592
  90.3 1.4 %copy.12 = bf16[3072,384]{1,0:T(8,128)(2,1)} copy(bf16[3072,384]{1,0:T(8,128)(2,1)S(1)} %get-tuple-element.11) | data formatting | bytes 4718592

commit v5 on v4

--- a/solution.py
+++ b/solution.py
@@ -373,6 +373,8 @@
         ]
         for copy in self.own:
             copy.start()
+
+    def load_weights(self):
         for i, src in enumerate((self.wu_in, self.wd_in)):
             for slot in range(8):
                 for other in range(2):
@@ -383,6 +385,7 @@
                     ).start()
 
     def own_wait(self):
+        self.load_weights()
         for copy in self.own:
             copy.wait()
 

time: 91.9 us -> 91.9 us (level)
  no operation moved by 1% of the time
where the time goes in v5:
time: 91.9 us; the launch traced here: 91.7 us
  Pallas kernels  87.6 us (95%)
  local copies, waits for them, and re-layouts  3.49 us (4%)
    pallas_call x1, Pallas kernels, on_device(): pl.pallas_call(kernel, out_shape=(pltpu.VMEM((192, 256), f32), pltpu.VMEM...  87.6 us
    unnamed x3, local copies, waits for them, and re-layouts  3.49 us

profile of v5, /device:TPU:2, one launch (start us, length us, event | category | flops | bytes accessed | tf_op | source)
XLA Modules:
  0.0 91.7 jit_solution(18234718058453075346)
XLA Ops:
  0.6 87.6 %ffn_backward.1 = (f32[192,256]{1,0:T(8,128)S(1)}, bf16[3072,384]{1,0:T(8,128)(2,1)S(1)}, bf16[3072,384]{1,0:T(8,128)(2,1)S(1)}) custom-call(bf16[192,256]{1,0:T(8,128)(2,1)} %bitcast.4, bf16[192,256]{1,0:T(8,128)(2,1)} %bitcast.5, bf16[3072,384]{1,0:T(8,128)(2,1)} %wu_in.1, bf16[3072,384]{1,0:T(8,128)(2,1)} %wd_in.1), custom_call_target="tpu_custom_call" | custom-call | flops 12079595520 | bytes 10000000 | tf_op jit(solution)/shard_map/ffn_backward/pallas_call | solution.py:616
  88.2 0.7 copy.10
  88.9 1.4 %copy.11 = bf16[3072,384]{1,0:T(8,128)(2,1)} copy(bf16[3072,384]{1,0:T(8,128)(2,1)S(1)} %get-tuple-element.10) | data formatting | bytes 4718592
  90.3 1.4 %copy.12 = bf16[3072,384]{1,0:T(8,128)(2,1)} copy(bf16[3072,384]{1,0:T(8,128)(2,1)S(1)} %get-tuple-element.11) | data formatting | bytes 4718592
